TPU v7x, 512 devices: a whole 4x4x16 slice. The times are simulated.
512 devices in a mesh: half: 2 (over core), row: 16 (over z), col: 16 (over y, x).
Axes of the slice: x: 4, y: 4, z: 16, core: 2. Of those that a mesh axis runs over, the one named last changes fastest.
Arguments:
- child_front: float32 [2, 8192, 8192], P('half', 'row', 'col'), as said below
- child_map: int32 [2, 48], P('half'), may hold values from 0 to 63, as said below
- root_front: float32 [8192, 16, 2, 256], P('row', 'col', 'half'), as said below
Outputs:
- child_panel: float32 [2, 512, 8192], P('half', None, 'col')
- root_panel: float32 [512, 16, 2, 256], P(None, 'col', 'half')
- root_update: float32 [8192, 16, 2, 256], P('row', 'col', 'half')
Inputs may be any that keep to these rules, and one draw needn't show every extreme that they name: `child_map`: for child h, the update blocks of row part k (the 3 blocks after that part's first block) map in increasing order to distinct blocks among the root's blocks k * 4 to (k + 1) * 4 - 1. `child_front`: each child's front is symmetric and positive definite. `root_front`: the root front is symmetric and positive definite.
All inputs are finite; a program needn't handle non-finite values.
Results may differ from a plain program's by a relative error of at most 0.0001.
Values sent between devices are 32-bit elements; how exact they have to be, the bound alone decides.
A program may use at most 64 MiB of HBM per device.

v0:
```python
import jax
import jax.numpy as jnp
from jax import lax
from jax.sharding import PartitionSpec as P

BLK = 128
PB = 32


def spread_2(value, axis, source):
    kept = jnp.where(lax.axis_index(axis) == source, value, 0).astype(value.dtype)
    return lax.psum(kept, axis)


def lower_solve(factor, right):
    return lax.linalg.triangular_solve(factor, right, left_side=True, lower=True)


def transposed_product(left, right):
    return lax.dot_general(
        left,
        right,
        (((0,), (0,)), ((), ())),
        precision=lax.Precision.HIGHEST,
        preferred_element_type=jnp.float32,
    )


def selector(child_row_map, part_index, child_tiles, root_tiles):
    per_part = child_tiles - 1
    targets = (
        lax.dynamic_slice_in_dim(child_row_map, part_index * per_part, per_part)
        - part_index * root_tiles
    )
    one_hot = (jnp.arange(root_tiles, dtype=jnp.int32)[:, None] == targets[None, :]).astype(
        jnp.float32
    )
    return jnp.concatenate([jnp.zeros((root_tiles, 1), jnp.float32), one_hot], axis=1)


def body(child_front, child_map, root_front):
    tile_rows = BLK
    pivot_count = PB
    child_block = child_front[0]
    part_rows = child_block.shape[0]
    row_part = lax.axis_index("row")
    col_part = lax.axis_index("col")
    strips = lax.all_gather(child_block[:pivot_count, :], "row", axis=0, tiled=True)
    pieces = lax.all_gather(
        child_block[None, :pivot_count, :pivot_count], ("row", "col"), axis=0, tiled=True
    )
    parts_count = lax.axis_size("row")
    corner = pieces.reshape(parts_count, parts_count, pivot_count, pivot_count).transpose(
        0, 2, 1, 3
    )
    corner = corner.reshape(parts_count * pivot_count, parts_count * pivot_count)
    factor = jnp.linalg.cholesky(corner)
    child_panel = lower_solve(factor, strips)
    columns = lax.all_gather(child_block[:, :pivot_count], "col", axis=1, tiled=True)
    panel_rows = lower_solve(factor, columns.T)
    update = child_block - transposed_product(panel_rows, child_panel)
    root_rows = root_front.shape[0]
    child_tiles = part_rows // tile_rows
    root_tiles = root_rows // tile_rows
    own_map = child_map[0]
    row_select = selector(own_map, row_part, child_tiles, root_tiles)
    col_select = selector(own_map, col_part, child_tiles, root_tiles)
    blocks = update.reshape(child_tiles, tile_rows, child_tiles, tile_rows)
    spread = jnp.einsum("ap,piqj->aiqj", row_select, blocks, precision=lax.Precision.HIGHEST)
    spread = jnp.einsum("aiqj,bq->aibj", spread, col_select, precision=lax.Precision.HIGHEST)
    additions = spread.reshape(root_rows, 2, root_rows // 2)
    joined = lax.psum_scatter(additions, "half", scatter_dimension=1, tiled=True)
    assembled = root_front[:, 0, 0, :] + joined[:, 0, :]
    root_strips = lax.all_gather(assembled[:pivot_count, :], "row", axis=0, tiled=True)
    pivots = spread_2(root_strips[:, :pivot_count], "half", 0)
    root_corner = lax.all_gather(pivots, "col", axis=1, tiled=True)
    root_factor = jnp.linalg.cholesky(root_corner)
    root_panel = lower_solve(root_factor, root_strips)
    mirrored = spread_2(root_panel, "col", row_part)
    both_halves = lax.all_gather(mirrored[:, None, :], "half", axis=1, tiled=True)
    panel_side = both_halves.reshape(both_halves.shape[0], root_rows)
    root_update = assembled - transposed_product(panel_side, root_panel)
    return (child_panel[None], root_panel[:, None, None, :], root_update[:, None, None, :])


def solution(mesh):
    return jax.shard_map(
        body,
        mesh=mesh,
        in_specs=(P("half", "row", "col"), P("half", None), P("row", "col", "half", None)),
        out_specs=(
            P("half", None, "col"),
            P(None, "col", "half", None),
            P("row", "col", "half", None),
        ),
        check_vma=False,
    )
```

profile of v0, /device:TPU:1, one launch (start us, length us, event | category | flops | bytes accessed | tf_op | source)
XLA Modules:
  0.0 844.2 jit_solution(4435899986150828886)
XLA Ops:
  12.8 208.7 %all-gather.14.cloned.1.call-done = f32[8192,32]{1,0:T(8,128)} async-done(((f32[32,32]{1,0:T(8,128)}), f32[8192,32]{1,0:T(8,128)}) %all-gather.14.cloned.1.call-update) | async-done | bytes 1048592 | tf_op jit(solution)/shard_map/all_gather | solution.py:49
  221.5 5.6 copy.23
  227.1 3.5 reshape.68
  232.2 11.7 %cholesky.286 = f32[128,128]{1,0:T(8,128)S(1)} custom-call(f32[128,128]{1,0:T(8,128)S(1)} %cholesky.426), custom_call_target="Cholesky" | custom-call | tf_op jit(solution)/shard_map/jit(cholesky)/cholesky | solution.py:57
  244.0 9.8 %custom-call.31 = f32[1,128,128]{1,2,0:T(8,128)S(1)} custom-call(f32[1,128,128]{2,1,0:T(8,128)S(1)} %get-tuple-element.79), custom_call_target="InvertDiagBlocksLowerTriangular" | custom-call | tf_op jit(solution)/shard_map/jit(cholesky)/cholesky | solution.py:57
  256.4 11.7 %cholesky.305 = f32[128,128]{1,0:T(8,128)S(1)} custom-call(f32[128,128]{1,0:T(8,128)S(1)} %cholesky.430), custom_call_target="Cholesky" | custom-call | tf_op jit(solution)/shard_map/jit(cholesky)/cholesky | solution.py:57
  268.2 10.0 %custom-call.32 = f32[1,128,128]{1,2,0:T(8,128)S(1)} custom-call(f32[1,128,128]{2,1,0:T(8,128)S(1)} %get-tuple-element.76), custom_call_target="InvertDiagBlocksLowerTriangular" | custom-call | tf_op jit(solution)/shard_map/jit(cholesky)/cholesky | solution.py:57
  279.7 11.7 %cholesky.326 = f32[128,128]{1,0:T(8,128)S(1)} custom-call(f32[128,128]{1,0:T(8,128)S(1)} %cholesky.435), custom_call_target="Cholesky" | custom-call | tf_op jit(solution)/shard_map/jit(cholesky)/cholesky | solution.py:57
  292.2 9.8 %custom-call.33 = f32[1,128,128]{1,2,0:T(8,128)S(1)} custom-call(f32[1,128,128]{2,1,0:T(8,128)S(1)} %get-tuple-element.73), custom_call_target="InvertDiagBlocksLowerTriangular" | custom-call | tf_op jit(solution)/shard_map/jit(cholesky)/cholesky | solution.py:57
  303.5 11.7 %cholesky.343 = f32[128,128]{1,0:T(8,128)S(1)} custom-call(f32[128,128]{1,0:T(8,128)S(1)} %convolution_subtract_fusion.16), custom_call_target="Cholesky" | custom-call | tf_op jit(solution)/shard_map/jit(cholesky)/cholesky | solution.py:57
  319.6 8.5 %while.6 = (s32[]{:T(128)}, f32[512,512]{1,0:T(8,128)S(1)}, s32[4,2]{0,1:T(2,128)S(1)}, f32[4,128,128]{2,1,0:T(8,128)S(1)}, s32[]{:T(128)}) while((s32[]{:T(128)}, f32[512,512]{1,0:T(8,128)S(1)}, s32[4,2]{0,1:T(2,128)S(1)}, f32[4,128,128]{2,1,0:T(8,128)S(1)}, s32[]{:T(128)}) %tuple.64), condition=%wide.while_cond, body=%wide.while_body.sunk | while | flops 2 | bytes 131181 | solution.py:16
  328.1 39.3 %custom-call.34 = f32[4,128,128]{1,2,0:T(8,128)S(1)} custom-call(f32[4,128,128]{2,1,0:T(8,128)S(1)} %get-tuple-element.27), custom_call_target="InvertDiagBlocksLowerTriangular" | custom-call | tf_op jit(solution)/shard_map/triangular_solve/custom-call.3 | solution.py:16
  373.1 1.6 convolution_subtract_fusion.6
  380.8 1.6 convolution_subtract_fusion.7
  383.6 3.1 convolution_subtract_fusion
  387.0 1.7 fusion.11
  392.0 23.3 %reduce-scatter.2.cloned.1.call-done = f32[512,1,256]{2,0,1:T(8,128)} async-done(((f32[512,2,256]{2,0,1:T(8,128)}), f32[512,1,256]{2,0,1:T(8,128)}) %reduce-scatter.2.cloned.1.call-update) | async-done | bytes 524304 | tf_op jit(solution)/shard_map/reduce_scatter | solution.py:72
  417.2 25.4 %all_gather.21 = f32[512,256]{1,0:T(8,128)S(1)} all-gather(f32[32,256]{1,0:T(8,128)S(1)} %slice.211), channel_id=1, replica_groups=mesh['half'=2,'row'=16,'col'=16] {'row'}, dimensions={0}, use_global_device_ids=true | all-gather | bytes 557056 | tf_op jit(solution)/shard_map/all_gather | solution.py:74
  443.4 44.3 %all-reduce.6.cloned.1.call-done = f32[512,32]{0,1:T(8,128)} async-done(((f32[512,32]{0,1:T(8,128)}), f32[512,32]{0,1:T(8,128)}) %all-reduce.6.cloned.1.call-update) | async-done | bytes 65552 | tf_op jit(solution)/shard_map/psum | solution.py:12
  487.9 59.6 %all-gather.10.cloned.1.call-done = f32[512,512]{0,1:T(8,128)} async-done(((f32[512,32]{0,1:T(8,128)}), f32[512,512]{0,1:T(8,128)}) %all-gather.10.cloned.1.call-update) | async-done | bytes 1048592 | tf_op jit(solution)/shard_map/all_gather | solution.py:76
  550.5 11.7 %cholesky.358 = f32[128,128]{1,0:T(8,128)S(1)} custom-call(f32[128,128]{1,0:T(8,128)S(1)} %cholesky.439), custom_call_target="Cholesky" | custom-call | tf_op jit(solution)/shard_map/jit(cholesky)/cholesky | solution.py:77
  562.4 9.8 %custom-call.36 = f32[1,128,128]{1,2,0:T(8,128)S(1)} custom-call(f32[1,128,128]{2,1,0:T(8,128)S(1)} %get-tuple-element.69), custom_call_target="InvertDiagBlocksLowerTriangular" | custom-call | tf_op jit(solution)/shard_map/jit(cholesky)/cholesky | solution.py:77
  573.6 11.7 %cholesky.377 = f32[128,128]{1,0:T(8,128)S(1)} custom-call(f32[128,128]{1,0:T(8,128)S(1)} %cholesky.443), custom_call_target="Cholesky" | custom-call | tf_op jit(solution)/shard_map/jit(cholesky)/cholesky | solution.py:77
  586.7 10.0 %custom-call.37 = f32[1,128,128]{1,2,0:T(8,128)S(1)} custom-call(f32[1,128,128]{2,1,0:T(8,128)S(1)} %get-tuple-element.66), custom_call_target="InvertDiagBlocksLowerTriangular" | custom-call | tf_op jit(solution)/shard_map/jit(cholesky)/cholesky | solution.py:77
  598.8 13.2 %cholesky.398 = f32[128,128]{1,0:T(8,128)} custom-call(f32[128,128]{1,0:T(8,128)} %cholesky.448), custom_call_target="Cholesky" | custom-call | tf_op jit(solution)/shard_map/jit(cholesky)/cholesky | solution.py:77
  614.2 11.3 %custom-call.38 = f32[1,128,128]{1,2,0:T(8,128)} custom-call(f32[1,128,128]{2,1,0:T(8,128)} %get-tuple-element.63), custom_call_target="InvertDiagBlocksLowerTriangular" | custom-call | tf_op jit(solution)/shard_map/jit(cholesky)/cholesky | solution.py:77
  626.9 11.7 %cholesky.415 = f32[128,128]{1,0:T(8,128)S(1)} custom-call(f32[128,128]{1,0:T(8,128)S(1)} %convolution_subtract_fusion.15), custom_call_target="Cholesky" | custom-call | tf_op jit(solution)/shard_map/jit(cholesky)/cholesky | solution.py:77
  642.2 8.0 while.5
  650.2 39.3 %custom-call.26 = f32[4,128,128]{1,2,0:T(8,128)S(1)} custom-call(f32[4,128,128]{2,1,0:T(8,128)S(1)} %get-tuple-element.20), custom_call_target="InvertDiagBlocksLowerTriangular" | custom-call | tf_op jit(solution)/shard_map/triangular_solve | solution.py:16
  693.7 115.5 %all-reduce.8.cloned.1.call-done = f32[512,1,256]{2,0,1:T(8,128)} async-done(((f32[512,1,256]{2,0,1:T(8,128)}), f32[512,1,256]{2,0,1:T(8,128)}) %all-reduce.8.cloned.1.call-update) | async-done | bytes 524304 | tf_op jit(solution)/shard_map/psum | solution.py:12
  809.2 2.0 fusion.23
  812.5 20.5 %all-gather.12.cloned.1.call-done = f32[512,2,256]{2,0,1:T(8,128)} async-done(((f32[512,1,256]{2,0,1:T(8,128)}), f32[512,2,256]{2,0,1:T(8,128)}) %all-gather.12.cloned.1.call-update) | async-done | bytes 1048592 | tf_op jit(solution)/shard_map/all_gather | solution.py:80
  (146 shorter events, 73.0 us)
Async XLA Ops:
  7.2 214.4 %all-gather.14.cloned.1.call-start = ((), (), s32[]{:S(2)}) async-start(), calls=%async_computation.7 | async-start | bytes 4210688 | tf_op jit(solution)/shard_map/all_gather | solution.py:49
  8.6 358.9 %all-gather.8.cloned.1.call-start = ((), (), s32[]{:S(2)}) async-start(), calls=%async_computation.1 | async-start | bytes 1114112 | tf_op jit(solution)/shard_map/all_gather | solution.py:59
  10.3 365.5 %all-gather.16.cloned.1.call-start = ((), (), s32[]{:S(2)}) async-start(), calls=%async_computation.8 | async-start | bytes 1114112 | tf_op jit(solution)/shard_map/all_gather | solution.py:48
  11.9 403.3 %reduce-scatter.2.cloned.1.call-start = ((), (), s32[]{:S(2)}) async-start(), calls=%async_computation.2 | async-start | bytes 1572864 | tf_op jit(solution)/shard_map/reduce_scatter | solution.py:72
  231.2 1.0 copy-start
  372.4 0.7 copy-start.3
  375.8 7.7 copy-start.4
  375.8 7.7 copy-start.9
  382.9 0.7 copy-start.5
  388.7 26.5 %copy-start.7 = (f32[512,1,1,256]{3,2,1,0:T(1,128)S(1)}, f32[512,1,1,256]{3,2,1,0:T(1,128)}, u32[]{:S(2)}) copy-start(f32[512,1,1,256]{3,2,1,0:T(1,128)} %param.8) | copy-start | bytes 1572868
  391.9 95.8 %all-reduce.6.cloned.1.call-start = ((), (), s32[]{:S(2)}) async-start(), calls=%async_computation.3 | async-start | bytes 131072 | tf_op jit(solution)/shard_map/psum | solution.py:12
  416.4 0.8 copy-start.1
  443.3 104.2 %all-gather.10.cloned.1.call-start = ((), (), s32[]{:S(2)}) async-start(), calls=%async_computation.4 | async-start | bytes 1114112 | tf_op jit(solution)/shard_map/all_gather | solution.py:76
  487.7 321.4 %all-reduce.8.cloned.1.call-start = ((), (), s32[]{:S(2)}) async-start(), calls=%async_computation.5 | async-start | bytes 1048576 | tf_op jit(solution)/shard_map/psum | solution.py:12
  572.9 0.7 copy-start.6
  689.6 1.5 copy-start.8
  691.5 143.1 %copy-start.2 = (f32[512,256]{1,0:T(8,128)S(1)}, f32[512,256]{1,0:T(8,128)}, u32[]{:S(2)}) copy-start(f32[512,256]{1,0:T(8,128)} %copy-done.1) | copy-start | bytes 1572868
  693.6 139.4 %all-gather.12.cloned.1.call-start = ((), (), s32[]{:S(2)}) async-start(), calls=%async_computation.6 | async-start | bytes 1572864 | tf_op jit(solution)/shard_map/all_gather | solution.py:80
Sparse Core Ops, SparseCore 0:
  13.1 208.4 all-gather.13
  225.1 59.4 all-gather.7
  287.2 63.2 all-gather.15
  392.0 23.1 reduce-scatter.1
  443.5 44.1 all-reduce.5
  491.0 56.4 all-gather.9
  693.7 115.3 all-reduce.7
  811.2 21.7 all-gather.11
where the time goes:
time: 855 us; the launch traced here: 844 us
  waiting for transfers between devices  472 us (55%)
  other arithmetic  248 us (29%)
  local copies, waits for them, and re-layouts  43.7 us (5%)
  matrix products  33.6 us (4%)
  blocking collectives  25.4 us (3%)
  between operations  20.3 us (2%)
    all_gather x1, waiting for transfers between devices, body(): lax.all_gather(child_block[None, :pivot_count, :pivot_count], ('row', 'co...  209 us
    psum x2, waiting for transfers between devices, spread_2(): return lax.psum(kept, axis)  160 us
    another operation x15, other arithmetic, body(): root_factor = jnp.linalg.cholesky(root_corner)  83.6 us
    another operation x5, other arithmetic, lower_solve(): lax.linalg.triangular_solve(factor, right, left_side=True, lower=True)  79.1 us
    another operation x14, other arithmetic, body(): factor = jnp.linalg.cholesky(corner)  78.6 us
    all_gather x1, waiting for transfers between devices, body(): root_corner = lax.all_gather(pivots, 'col', axis=1, tiled=True)  59.6 us
    all_gather x1, blocking collectives, body(): lax.all_gather(assembled[:pivot_count, :], 'row', axis=0, tiled=True)  25.4 us
    reduce_scatter x1, waiting for transfers between devices, body(): lax.psum_scatter(additions, 'half', scatter_dimension=1, tiled=True)  23.3 us
  transfers between devices with their start and end apart: 8, of which 6 were waited for; matrix products, arithmetic and copies ran while one was open for 19% of the time, Pallas kernels for 0%

commit v1 on v0

--- a/solution.py
+++ b/solution.py
@@ -9,7 +9,7 @@
 
 def spread_2(value, axis, source):
     kept = jnp.where(lax.axis_index(axis) == source, value, 0).astype(value.dtype)
-    return lax.psum(kept, axis)
+    return jnp.sum(lax.all_gather(kept, axis), axis=0)
 
 
 def lower_solve(factor, right):

time: 855 us -> 787 us (0.920)
  waiting for transfers between devices: 472 us -> 391 us
  blocking collectives: 25.4 us -> 34.6 us
    psum x2 -> x0, waiting for transfers between devices: 160 us -> none  [spread_2(): return lax.psum(kept, axis)]
    all_gather x0 -> x1, waiting for transfers between devices: none -> 86.9 us  [spread_2(): return jnp.sum(lax.all_gather(kept, axis), axis=0)]
    all_gather x0 -> x1, blocking collectives: none -> 9.2 us  [spread_2(): return jnp.sum(lax.all_gather(kept, axis), axis=0)]
  transfers between devices with their start and end apart: 8 -> 7, of which waited for: 6 -> 5; matrix products, arithmetic and copies ran while one was open for 19% -> 20% of each run, Pallas kernels for 0% -> 0%
where the time goes in v1:
time: 787 us; the launch traced here: 776 us
  waiting for transfers between devices  391 us (50%)
  other arithmetic  248 us (32%)
  local copies, waits for them, and re-layouts  44.8 us (6%)
  matrix products  35.9 us (5%)
  blocking collectives  34.6 us (4%)
  between operations  20.2 us (3%)
    all_gather x1, waiting for transfers between devices, body(): lax.all_gather(child_block[None, :pivot_count, :pivot_count], ('row', 'co...  209 us
    all_gather x1, waiting for transfers between devices, spread_2(): return jnp.sum(lax.all_gather(kept, axis), axis=0)  86.9 us
    another operation x5, other arithmetic, lower_solve(): lax.linalg.triangular_solve(factor, right, left_side=True, lower=True)  80.1 us
    another operation x15, other arithmetic, body(): root_factor = jnp.linalg.cholesky(root_corner)  79.2 us
    another operation x14, other arithmetic, body(): factor = jnp.linalg.cholesky(corner)  78.6 us
    all_gather x1, waiting for transfers between devices, body(): root_corner = lax.all_gather(pivots, 'col', axis=1, tiled=True)  53.4 us
    all_gather x1, blocking collectives, body(): lax.all_gather(assembled[:pivot_count, :], 'row', axis=0, tiled=True)  25.4 us
    reduce_scatter x1, waiting for transfers between devices, body(): lax.psum_scatter(additions, 'half', scatter_dimension=1, tiled=True)  23.3 us
  transfers between devices with their start and end apart: 7, of which 5 were waited for; matrix products, arithmetic and copies ran while one was open for 20% of the time, Pallas kernels for 0%

profile of v1, /device:TPU:1, one launch (start us, length us, event | category | flops | bytes accessed | tf_op | source)
XLA Modules:
  0.0 776.0 jit_solution(6063292462937032915)
XLA Ops:
  12.8 208.7 %all-gather.17.cloned.1.call-done = f32[8192,32]{1,0:T(8,128)} async-done(((f32[32,32]{1,0:T(8,128)}), f32[8192,32]{1,0:T(8,128)}) %all-gather.17.cloned.1.call-update) | async-done | bytes 1048592 | tf_op jit(solution)/shard_map/all_gather | solution.py:49
  221.5 5.6 copy.12
  227.1 3.5 reshape.123
  231.3 11.7 %cholesky.286 = f32[128,128]{1,0:T(8,128)S(1)} custom-call(f32[128,128]{1,0:T(8,128)S(1)} %cholesky.426), custom_call_target="Cholesky" | custom-call | tf_op jit(solution)/shard_map/jit(cholesky)/cholesky | solution.py:57
  243.0 9.8 %custom-call.31 = f32[1,128,128]{1,2,0:T(8,128)S(1)} custom-call(f32[1,128,128]{2,1,0:T(8,128)S(1)} %get-tuple-element.74), custom_call_target="InvertDiagBlocksLowerTriangular" | custom-call | tf_op jit(solution)/shard_map/jit(cholesky)/cholesky | solution.py:57
  253.6 11.7 %cholesky.305 = f32[128,128]{1,0:T(8,128)S(1)} custom-call(f32[128,128]{1,0:T(8,128)S(1)} %cholesky.430), custom_call_target="Cholesky" | custom-call | tf_op jit(solution)/shard_map/jit(cholesky)/cholesky | solution.py:57
  265.4 10.0 %custom-call.32 = f32[1,128,128]{1,2,0:T(8,128)S(1)} custom-call(f32[1,128,128]{2,1,0:T(8,128)S(1)} %get-tuple-element.71), custom_call_target="InvertDiagBlocksLowerTriangular" | custom-call | tf_op jit(solution)/shard_map/jit(cholesky)/cholesky | solution.py:57
  276.0 11.7 %cholesky.326 = f32[128,128]{1,0:T(8,128)S(1)} custom-call(f32[128,128]{1,0:T(8,128)S(1)} %cholesky.435), custom_call_target="Cholesky" | custom-call | tf_op jit(solution)/shard_map/jit(cholesky)/cholesky | solution.py:57
  288.5 9.8 %custom-call.33 = f32[1,128,128]{1,2,0:T(8,128)S(1)} custom-call(f32[1,128,128]{2,1,0:T(8,128)S(1)} %get-tuple-element.68), custom_call_target="InvertDiagBlocksLowerTriangular" | custom-call | tf_op jit(solution)/shard_map/jit(cholesky)/cholesky | solution.py:57
  298.9 11.7 %cholesky.343 = f32[128,128]{1,0:T(8,128)S(1)} custom-call(f32[128,128]{1,0:T(8,128)S(1)} %convolution_subtract_fusion.16), custom_call_target="Cholesky" | custom-call | tf_op jit(solution)/shard_map/jit(cholesky)/cholesky | solution.py:57
  314.6 8.9 %while.6 = (s32[]{:T(128)}, f32[512,512]{1,0:T(8,128)S(1)}, s32[4,2]{0,1:T(2,128)S(1)}, f32[4,128,128]{2,1,0:T(8,128)S(1)}, s32[]{:T(128)}) while((s32[]{:T(128)}, f32[512,512]{1,0:T(8,128)S(1)}, s32[4,2]{0,1:T(2,128)S(1)}, f32[4,128,128]{2,1,0:T(8,128)S(1)}, s32[]{:T(128)}) %tuple.62), condition=%wide.while_cond, body=%wide.while_body.sunk | while | flops 2 | bytes 131181 | solution.py:16
  323.5 39.3 %custom-call.34 = f32[4,128,128]{1,2,0:T(8,128)S(1)} custom-call(f32[4,128,128]{2,1,0:T(8,128)S(1)} %get-tuple-element.27), custom_call_target="InvertDiagBlocksLowerTriangular" | custom-call | tf_op jit(solution)/shard_map/triangular_solve/custom-call.3 | solution.py:16
  377.5 4.0 convolution_subtract_fusion
  388.1 23.3 %reduce-scatter.2.cloned.1.call-done = f32[512,1,256]{2,0,1:T(8,128)} async-done(((f32[512,2,256]{2,0,1:T(8,128)}), f32[512,1,256]{2,0,1:T(8,128)}) %reduce-scatter.2.cloned.1.call-update) | async-done | bytes 524304 | tf_op jit(solution)/shard_map/reduce_scatter | solution.py:72
  412.6 25.4 %all_gather.31 = f32[512,256]{1,0:T(8,128)S(1)} all-gather(f32[32,256]{1,0:T(8,128)S(1)} %slice.211), channel_id=1, replica_groups=mesh['half'=2,'row'=16,'col'=16] {'row'}, dimensions={0}, use_global_device_ids=true | all-gather | bytes 557056 | tf_op jit(solution)/shard_map/all_gather | solution.py:74
  438.1 9.2 %all-gather.2 = f32[1024,32]{1,0:T(8,128)S(1)} all-gather(f32[512,32]{1,0:T(8,128)S(1)} %slice_select_fusion), channel_id=4, replica_groups=mesh['half'=2,'row'=16,'col'=16] {'half'}, dimensions={0}, use_global_device_ids=true | all-gather | bytes 196608 | tf_op jit(solution)/shard_map/all_gather | solution.py:12
  448.3 53.4 %all-gather.13.cloned.1.call-done = f32[512,512]{0,1:T(8,128)} async-done(((f32[512,32]{0,1:T(8,128)}), f32[512,512]{0,1:T(8,128)}) %all-gather.13.cloned.1.call-update) | async-done | bytes 1048592 | tf_op jit(solution)/shard_map/all_gather | solution.py:76
  505.7 11.7 %cholesky.358 = f32[128,128]{1,0:T(8,128)S(1)} custom-call(f32[128,128]{1,0:T(8,128)S(1)} %cholesky.439), custom_call_target="Cholesky" | custom-call | tf_op jit(solution)/shard_map/jit(cholesky)/cholesky | solution.py:77
  517.6 9.8 %custom-call.36 = f32[1,128,128]{1,2,0:T(8,128)S(1)} custom-call(f32[1,128,128]{2,1,0:T(8,128)S(1)} %get-tuple-element.64), custom_call_target="InvertDiagBlocksLowerTriangular" | custom-call | tf_op jit(solution)/shard_map/jit(cholesky)/cholesky | solution.py:77
  529.9 11.7 %cholesky.377 = f32[128,128]{1,0:T(8,128)S(1)} custom-call(f32[128,128]{1,0:T(8,128)S(1)} %cholesky.443), custom_call_target="Cholesky" | custom-call | tf_op jit(solution)/shard_map/jit(cholesky)/cholesky | solution.py:77
  543.1 10.0 %custom-call.37 = f32[1,128,128]{1,2,0:T(8,128)S(1)} custom-call(f32[1,128,128]{2,1,0:T(8,128)S(1)} %get-tuple-element.61), custom_call_target="InvertDiagBlocksLowerTriangular" | custom-call | tf_op jit(solution)/shard_map/jit(cholesky)/cholesky | solution.py:77
  554.6 11.7 %cholesky.398 = f32[128,128]{1,0:T(8,128)S(1)} custom-call(f32[128,128]{1,0:T(8,128)S(1)} %cholesky.448), custom_call_target="Cholesky" | custom-call | tf_op jit(solution)/shard_map/jit(cholesky)/cholesky | solution.py:77
  567.0 9.8 %custom-call.38 = f32[1,128,128]{1,2,0:T(8,128)S(1)} custom-call(f32[1,128,128]{2,1,0:T(8,128)S(1)} %get-tuple-element.58), custom_call_target="InvertDiagBlocksLowerTriangular" | custom-call | tf_op jit(solution)/shard_map/jit(cholesky)/cholesky | solution.py:77
  578.3 11.7 %cholesky.415 = f32[128,128]{1,0:T(8,128)S(1)} custom-call(f32[128,128]{1,0:T(8,128)S(1)} %convolution_subtract_fusion.15), custom_call_target="Cholesky" | custom-call | tf_op jit(solution)/shard_map/jit(cholesky)/cholesky | solution.py:77
  594.6 12.0 %while.5 = (s32[]{:T(128)}, f32[512,512]{1,0:T(8,128)}, s32[4,2]{0,1:T(2,128)S(1)}, f32[4,128,128]{2,1,0:T(8,128)S(1)}, s32[]{:T(128)}) while((s32[]{:T(128)}, f32[512,512]{1,0:T(8,128)}, s32[4,2]{0,1:T(2,128)S(1)}, f32[4,128,128]{2,1,0:T(8,128)S(1)}, s32[]{:T(128)}) %tuple.82), condition=%wide.while_cond.1, body=%wide.while_body.1.sunk | while | flops 2 | bytes 131181 | solution.py:16
  595.2 2.3 bitcast_dynamic-update-slice_fusion.4
  598.3 2.3 bitcast_dynamic-update-slice_fusion.4
  606.6 39.3 %custom-call.26 = f32[4,128,128]{1,2,0:T(8,128)S(1)} custom-call(f32[4,128,128]{2,1,0:T(8,128)S(1)} %get-tuple-element.20), custom_call_target="InvertDiagBlocksLowerTriangular" | custom-call | tf_op jit(solution)/shard_map/triangular_solve | solution.py:16
  651.7 86.9 %all-gather.15.cloned.1.call-done = f32[16,512,256]{2,1,0:T(8,128)} async-done(((f32[1,512,256]{2,1,0:T(8,128)}), f32[16,512,256]{2,1,0:T(8,128)}) %all-gather.15.cloned.1.call-update) | async-done | bytes 8388624 | tf_op jit(solution)/shard_map/all_gather | solution.py:12
  738.7 4.8 reduce_sum.19
  745.9 18.5 %all-gather.21.cloned.1.call-done = f32[512,512]{1,0:T(8,128)} async-done(((f32[512,256]{1,0:T(8,128)}), f32[512,512]{1,0:T(8,128)}) %all-gather.21.cloned.1.call-update) | async-done | bytes 1048592 | tf_op jit(solution)/shard_map/all_gather | solution.py:80
  764.4 3.0 fusion
  (131 shorter events, 72.6 us)
Async XLA Ops:
  7.2 214.4 %all-gather.17.cloned.1.call-start = ((), (), s32[]{:S(2)}) async-start(), calls=%async_computation.5 | async-start | bytes 4210688 | tf_op jit(solution)/shard_map/all_gather | solution.py:49
  8.6 354.3 %all-gather.11.cloned.1.call-start = ((), (), s32[]{:S(2)}) async-start(), calls=%async_computation.1 | async-start | bytes 1114112 | tf_op jit(solution)/shard_map/all_gather | solution.py:59
  10.3 359.5 %all-gather.19.cloned.1.call-start = ((), (), s32[]{:S(2)}) async-start(), calls=%async_computation.6 | async-start | bytes 1114112 | tf_op jit(solution)/shard_map/all_gather | solution.py:48
  11.9 399.4 %reduce-scatter.2.cloned.1.call-start = ((), (), s32[]{:S(2)}) async-start(), calls=%async_computation.2 | async-start | bytes 1572864 | tf_op jit(solution)/shard_map/reduce_scatter | solution.py:72
  376.8 0.7 copy-start.1
  388.0 113.7 %all-gather.13.cloned.1.call-start = ((), (), s32[]{:S(2)}) async-start(), calls=%async_computation.3 | async-start | bytes 1114112 | tf_op jit(solution)/shard_map/all_gather | solution.py:76
  448.1 290.6 %all-gather.15.cloned.1.call-start = ((), (), s32[]{:S(2)}) async-start(), calls=%async_computation.4 | async-start | bytes 8912896 | tf_op jit(solution)/shard_map/all_gather | solution.py:12
  504.7 1.0 copy-start
  651.7 91.8 %copy-start.2 = (f32[128,512]{1,0:T(8,128)S(1)}, f32[128,512]{1,0:T(8,128)}, u32[]{:S(2)}) copy-start(f32[128,512]{1,0:T(8,128)} %copy-done.1) | copy-start | bytes 786436
  651.7 112.7 %all-gather.21.cloned.1.call-start = ((), (), s32[]{:S(2)}) async-start(), calls=%async_computation.7 | async-start | bytes 1572864 | tf_op jit(solution)/shard_map/all_gather | solution.py:80
Sparse Core Ops, SparseCore 0:
  13.1 208.4 all-gather.16
  225.1 59.6 all-gather.10
  287.5 62.4 all-gather.18
  388.1 23.1 reduce-scatter.1
  448.2 53.4 all-gather.12
  651.8 86.8 all-gather.14
  743.6 20.7 all-gather.20
